TPU v7x, 32 devices: a whole 2x2x4 slice. The times are simulated.
32 devices in a mesh: groups: 2 (over y), dp: 4 (over z), owner: 2 (over x), seq: 2 (over core).
Axes of the slice: x: 2, y: 2, z: 4, core: 2. Of those that a mesh axis runs over, the one named last changes fastest.
Arguments:
- tokens: bfloat16 [4096, 6144], P(('groups', 'dp', 'seq')), parts along dimension 0, may hold values from -16 to 16
- document_lengths: int32 [8, 4], P(('groups', 'dp')), parts along dimension 0, may hold values from 1 to 384, 512 in all within a row
- document_adapter: int32 [8, 4], P(('groups', 'dp')), parts along dimension 0, may hold values from 0 to 3
- adapter_stored_row: int32 [4], replicated, may hold values from 0 to 3, each once
- query_weight: bfloat16 [6144, 3072], P('dp', 'owner'), may hold values from -0.078125 to 0.078125
- key_weight: bfloat16 [6144, 512], P('dp', 'owner'), may hold values from -0.078125 to 0.078125
- value_weight: bfloat16 [6144, 512], P('dp', 'owner'), may hold values from -0.078125 to 0.078125
- adapter_down_weight: bfloat16 [4, 6144, 8], P('dp', 'owner'), may hold values from -0.078125 to 0.078125
- adapter_up_weight: bfloat16 [4, 8, 3072], P('dp', None, 'owner'), may hold values from -2 to 2
- output_cotangent: bfloat16 [4096, 3072], P(('groups', 'dp', 'seq'), 'owner'), parts along dimension 0, may hold values from -6 to 6
Outputs:
- attended: bfloat16 [4096, 3072], P(('groups', 'dp', 'seq'), 'owner'), parts along dimension 0
- grad_down: float32 [8, 6144, 8], P(('groups', 'dp'), ('owner', 'seq')), parts along dimension 0
- grad_up: float32 [8, 8, 3072], P(('groups', 'dp'), None, ('owner', 'seq')), parts along dimension 0
There are 2 independent parts, one for each index of `groups`. A program takes and returns all parts, laid end to end along the dimension named above; an argument that names none is the same for every part. Nothing has to cross between parts.
Inputs may be any that keep to these rules, and one draw needn't show every extreme that they name: `document_lengths`: the 4 lengths of one sequence sum to 512. `adapter_stored_row`: each of the 4 stored rows once.
All inputs are finite; a program needn't handle non-finite values.
Results may differ from a plain program's by a relative error of at most 0.0085.
The roundings to bfloat16 on the way count: a program that leaves them out, or rounds other values in their place, can miss the bound.
Values may be sent and summed in bfloat16 or wider, within the bound.
A program may use at most 128 MiB of HBM per device.

v0:
```python
import math

import jax
import jax.numpy as jnp
from jax import lax
from jax.sharding import PartitionSpec as P

HEAD_SIZE = 128


rope_base = 1000000.0
neg_big = -1e30


def rotary_apply(rotated_in, token_positions, direction):
    half_width = rotated_in.shape[-1] // 2
    frequency = rope_base ** (
        -(jnp.arange(half_width).astype(jnp.float32) * 2.0 / rotated_in.shape[-1])
    )
    angles = token_positions.astype(jnp.float32)[:, None] * frequency[None, :]
    cosines = jnp.cos(angles)[:, None, :]
    sines = direction * jnp.sin(angles)[:, None, :]
    front_half = rotated_in[..., :half_width]
    back_half = rotated_in[..., half_width:]
    return jnp.concatenate(
        [front_half * cosines - back_half * sines, back_half * cosines + front_half * sines],
        axis=-1,
    )


def doc_number(token_positions, doc_ends):
    return jnp.sum((token_positions[:, None] >= doc_ends[None, :]).astype(jnp.int32), axis=1)


def shards(
    tokens,
    document_lengths,
    document_adapter,
    adapter_stored_row,
    query_weight,
    key_weight,
    value_weight,
    adapter_down_weight,
    adapter_up_weight,
    output_cotangent,
):
    row_count = tokens.shape[0]
    quarter_part = adapter_down_weight.shape[1]
    adapter_rank_size = adapter_down_weight.shape[2]
    query_cols = query_weight.shape[1]
    key_cols = key_weight.shape[1]
    head_count = query_cols // HEAD_SIZE
    key_heads = key_cols // HEAD_SIZE
    head_grouping = head_count // key_heads
    doc_count = document_lengths.shape[1]
    seq_devices = lax.axis_size("seq")
    adapters = lax.axis_size("dp")
    seq_at = lax.axis_index("seq")
    owner_at = lax.axis_index("owner")
    score_scale = 1.0 / math.sqrt(HEAD_SIZE)
    doc_ends = jnp.cumsum(document_lengths[0])
    own_positions = seq_at * row_count + jnp.arange(row_count, dtype=jnp.int32)
    doc_mine = doc_number(own_positions, doc_ends)
    in_document = doc_mine[:, None] == jnp.arange(doc_count, dtype=jnp.int32)[None, :]
    adapter_of = jnp.sum(jnp.where(in_document, document_adapter[0][None, :], 0), axis=1)
    adapter_ids = jnp.arange(adapters, dtype=jnp.int32)
    stored_row = jnp.sum(
        jnp.where(adapter_of[:, None] == adapter_ids[None, :], adapter_stored_row[None, :], 0),
        axis=1,
    )
    chooser = (stored_row[:, None] == adapter_ids[None, :]).astype(jnp.float32)
    base_query = jnp.dot(
        tokens,
        lax.all_gather(query_weight, "dp", axis=0, tiled=True),
        preferred_element_type=jnp.float32,
    )
    base_key = jnp.dot(
        tokens,
        lax.all_gather(key_weight, "dp", axis=0, tiled=True),
        preferred_element_type=jnp.float32,
    )
    base_value = jnp.dot(
        tokens,
        lax.all_gather(value_weight, "dp", axis=0, tiled=True),
        preferred_element_type=jnp.float32,
    )
    stored = (
        lax.all_gather(adapter_down_weight, "dp", axis=0, tiled=True),
        lax.all_gather(adapter_up_weight, "dp", axis=0, tiled=True),
    )
    up_weight_flat = stored[1].reshape(adapters * adapter_rank_size, query_cols)
    token_quarter = lax.dynamic_slice_in_dim(tokens, owner_at * quarter_part, quarter_part, 1)
    down_weight_flat = jnp.transpose(stored[0], (1, 0, 2)).reshape(
        quarter_part, adapters * adapter_rank_size
    )
    every_low = jnp.dot(
        token_quarter, down_weight_flat, preferred_element_type=jnp.float32
    ).reshape(row_count, adapters, adapter_rank_size)
    partial_low = jnp.sum(every_low * chooser[:, :, None], axis=1)
    low_rank = lax.psum(partial_low, "owner").astype(jnp.bfloat16)
    spread = (
        (low_rank.astype(jnp.float32)[:, None, :] * chooser[:, :, None])
        .astype(jnp.bfloat16)
        .reshape(row_count, adapters * adapter_rank_size)
    )
    query_raw = base_query + jnp.dot(spread, up_weight_flat, preferred_element_type=jnp.float32)
    query_rows = rotary_apply(
        query_raw.reshape(row_count, head_count, HEAD_SIZE), own_positions, 1.0
    ).astype(jnp.bfloat16)
    key_rows = rotary_apply(
        base_key.reshape(row_count, key_heads, HEAD_SIZE), own_positions, 1.0
    ).astype(jnp.bfloat16)
    value_rows = base_value.astype(jnp.bfloat16).reshape(row_count, key_heads, HEAD_SIZE)
    key_value = (
        lax.all_gather(key_rows, "seq", axis=0, tiled=True),
        lax.all_gather(value_rows, "seq", axis=0, tiled=True),
    )
    keys_seen = key_value[0]
    values_seen = key_value[1]
    key_positions = jnp.arange(row_count * seq_devices, dtype=jnp.int32)
    key_docs = doc_number(key_positions, doc_ends)
    allowed = (
        (key_docs[None, :] == doc_mine[:, None])
        & (key_positions[None, :] <= own_positions[:, None])
        & (key_positions[None, :] >= 0)
    )
    query_groups = query_rows.reshape(row_count, key_heads, head_grouping, HEAD_SIZE)
    output_gradient = output_cotangent.reshape(row_count, key_heads, head_grouping, HEAD_SIZE)
    scores = (
        jnp.einsum("qcgd,kcd->cgqk", query_groups, keys_seen, preferred_element_type=jnp.float32)
        * score_scale
    )
    scores = jnp.where(allowed[None, None], scores, neg_big)
    row_max = jnp.max(scores, axis=-1, keepdims=True)
    raised = jnp.exp(scores - row_max)
    probability = raised / jnp.sum(raised, axis=-1, keepdims=True)
    weights = probability.astype(jnp.bfloat16)
    attended = jnp.einsum(
        "cgqk,kcd->qcgd", weights, values_seen, preferred_element_type=jnp.float32
    )
    attended = attended.astype(jnp.bfloat16).reshape(row_count, query_cols)
    dprob = jnp.einsum(
        "qcgd,kcd->cgqk", output_gradient, values_seen, preferred_element_type=jnp.float32
    )
    row_delta = jnp.sum(probability * dprob, axis=-1, keepdims=True)
    dscore = (probability * (dprob - row_delta)).astype(jnp.bfloat16)
    grad_rot = (
        jnp.einsum("cgqk,kcd->qcgd", dscore, keys_seen, preferred_element_type=jnp.float32)
        * score_scale
    )
    grad_query = rotary_apply(
        grad_rot.reshape(row_count, head_count, HEAD_SIZE), own_positions, -1.0
    ).astype(jnp.bfloat16)
    grad_query = grad_query.reshape(row_count, query_cols)
    every_mid = lax.dot_general(
        grad_query, up_weight_flat, (((1,), (1,)), ((), ())), preferred_element_type=jnp.float32
    )
    partial_mid = jnp.sum(
        every_mid.reshape(row_count, adapters, adapter_rank_size) * chooser[:, :, None], axis=1
    )
    mid_rank = lax.psum(partial_mid, "owner").astype(jnp.bfloat16)
    spread_mid = (
        (mid_rank.astype(jnp.float32)[:, None, :] * chooser[:, :, None])
        .astype(jnp.bfloat16)
        .reshape(row_count, adapters * adapter_rank_size)
    )
    down_term = lax.dot_general(
        token_quarter, spread_mid, (((0,), (0,)), ((), ())), preferred_element_type=jnp.float32
    )
    down_term = jnp.transpose(
        down_term.reshape(quarter_part, adapters, adapter_rank_size), (1, 0, 2)
    )
    up_term = lax.dot_general(
        spread, grad_query, (((0,), (0,)), ((), ())), preferred_element_type=jnp.float32
    )
    up_term = up_term.reshape(adapters, adapter_rank_size, query_cols)
    down_term = down_term.reshape(
        adapters * seq_devices, quarter_part // seq_devices, adapter_rank_size
    )
    up_term = up_term.reshape(adapters, adapter_rank_size, seq_devices, query_cols // seq_devices)
    up_term = jnp.transpose(up_term, (0, 2, 1, 3)).reshape(
        adapters * seq_devices, adapter_rank_size, query_cols // seq_devices
    )
    gradients = (
        lax.psum_scatter(down_term, ("dp", "seq"), scatter_dimension=0, tiled=True),
        lax.psum_scatter(up_term, ("dp", "seq"), scatter_dimension=0, tiled=True),
    )
    return (attended, gradients[0], gradients[1])


def solution(mesh):
    in_specs = (
        P(("groups", "dp", "seq"), None),
        P(("groups", "dp"), None),
        P(("groups", "dp"), None),
        P(),
        P("dp", "owner"),
        P("dp", "owner"),
        P("dp", "owner"),
        P("dp", "owner", None),
        P("dp", None, "owner"),
        P(("groups", "dp", "seq"), "owner"),
    )
    out_specs = (
        P(("groups", "dp", "seq"), "owner"),
        P(("groups", "dp"), ("owner", "seq"), None),
        P(("groups", "dp"), None, ("owner", "seq")),
    )
    return jax.shard_map(shards, mesh=mesh, in_specs=in_specs, out_specs=out_specs, check_vma=False)
```

profile of v0, /device:TPU:0, one launch (start us, length us, event | category | flops | bytes accessed | tf_op | source)
XLA Modules:
  0.0 562.8 jit_solution(18081054362020784550)
XLA Ops:
  9.7 15.9 %all_gather.26 = bf16[4,3072,8]{1,2,0:T(8,128)(2,1)S(1)} all-gather(bf16[1,3072,8]{1,2,0:T(8,128)(2,1)S(1)} %copy-done.12), channel_id=1, replica_groups=mesh['groups'=2,'dp'=4,'owner'=2,'seq'=2] {'dp'}, dimensions={0}, use_global_device_ids=true | all-gather | bytes 245760 | tf_op jit(solution)/shard_map/all_gather | solution.py:88
  26.4 5.0 psum.14
  33.9 2.3 copy.82
  36.2 14.6 %all_gather.27 = bf16[4,8,1536]{2,1,0:T(8,128)(2,1)S(1)} all-gather(bf16[1,8,1536]{2,1,0:T(8,128)(2,1)S(1)} %copy-done.13), channel_id=1, replica_groups=mesh['groups'=2,'dp'=4,'owner'=2,'seq'=2] {'dp'}, dimensions={0}, use_global_device_ids=true | all-gather | bytes 122880 | tf_op jit(solution)/shard_map/all_gather | solution.py:89
  51.5 1.6 convolution_bitcast_fusion
  53.9 23.9 %all-gather.6.cloned.1.call-done = bf16[6144,256]{1,0:T(8,128)(2,1)} async-done(((bf16[1536,256]{1,0:T(8,128)(2,1)}), bf16[6144,256]{1,0:T(8,128)(2,1)}) %all-gather.6.cloned.1.call-update) | async-done | bytes 3145744 | tf_op jit(solution)/shard_map/all_gather | solution.py:79
  77.8 3.2 fusion.63
  81.8 1.0 copy.103
  83.6 1.2 subtract_convert_fusion.2
  84.9 2.1 all_gather.24
  87.0 54.4 %all-gather.4.cloned.1.call-done = bf16[6144,256]{1,0:T(8,128)(2,1)} async-done(((bf16[1536,256]{1,0:T(8,128)(2,1)}), bf16[6144,256]{1,0:T(8,128)(2,1)}) %all-gather.4.cloned.1.call-update) | async-done | bytes 3145744 | tf_op jit(solution)/shard_map/all_gather | solution.py:84
  141.4 3.2 convolution_convert_fusion
  144.6 2.3 all_gather.22
  146.9 317.3 %all-gather.8.cloned.1.call-done = bf16[6144,1536]{1,0:T(8,128)(2,1)} async-done(((bf16[1536,1536]{1,0:T(8,128)(2,1)}), bf16[6144,1536]{1,0:T(8,128)(2,1)}) %all-gather.8.cloned.1.call-update) | async-done | bytes 18874384 | tf_op jit(solution)/shard_map/all_gather | solution.py:74
  464.3 10.8 %convolution_add_fusion = f32[256,1536]{1,0:T(8,128)} fusion(f32[256,1536]{1,0:T(8,128)} %convolution_bitcast_fusion, bf16[256,6144]{1,0:T(8,128)(2,1)S(1)} %copy-done, bf16[6144,1536]{1,0:T(8,128)(2,1)} %all-gather.8.cloned.1.call-done), kind=kOutput, calls=%fused_computation.17 | convolution fusion | flops 4832231424 | bytes 25165824 | tf_op jit(solution)/shard_map/dot_general | solution.py:72
  475.1 3.0 copy.78
  478.1 2.3 subtract_convert_fusion.1
  480.5 2.1 copy.79
  482.6 1.2 copy.80
  483.8 2.5 fusion.32
  486.4 2.7 fusion.62
  489.1 1.1 fusion.1
  490.2 1.5 copy-done.17
  491.7 1.4 fusion.17
  494.3 1.0 fusion.44
  495.4 1.4 fusion.28
  496.8 5.0 psum.15
  501.8 1.1 fusion.13
  503.0 4.3 fusion.20
  507.3 2.3 copy.88
  509.5 15.1 %reduce-scatter.5.cloned.1.call-done = f32[1,8,768]{2,1,0:T(8,128)} async-done(((f32[8,8,768]{2,1,0:T(8,128)}), f32[1,8,768]{2,1,0:T(8,128)}) %reduce-scatter.5.cloned.1.call-update) | async-done | bytes 24592 | tf_op jit(solution)/shard_map/reduce_scatter | solution.py:186
  524.6 31.6 %reduce-scatter.3.cloned.1.call-done = f32[1,1536,8]{1,2,0:T(8,128)} async-done(((f32[8,1536,8]{1,2,0:T(8,128)}), f32[1,1536,8]{1,2,0:T(8,128)}) %reduce-scatter.3.cloned.1.call-update) | async-done | bytes 49168 | tf_op jit(solution)/shard_map/reduce_scatter | solution.py:185
  (66 shorter events, 10.1 us)
Async XLA Ops:
  7.2 18.7 %copy-start = (bf16[256,6144]{1,0:T(8,128)(2,1)S(1)}, bf16[256,6144]{1,0:T(8,128)(2,1)}, u32[]{:S(2)}) copy-start(bf16[256,6144]{1,0:T(8,128)(2,1)} %param.10) | copy-start | bytes 9437188
  7.2 2.3 copy-start.16
  7.2 2.5 copy-start.12
  7.2 18.5 %copy-start.14 = (s32[1,4]{1,0:T(1,128)S(1)}, s32[1,4]{1,0:T(1,128)}, u32[]{:S(2)}) copy-start(s32[1,4]{1,0:T(1,128)} %param.12) | copy-start | bytes 52
  7.2 18.6 %copy-start.15 = (s32[4]{0:T(128)S(1)}, s32[4]{0:T(128)}, u32[]{:S(2)}) copy-start(s32[4]{0:T(128)} %param.13) | copy-start | bytes 52
  7.2 70.6 %all-gather.6.cloned.1.call-start = ((), (), s32[]{:S(2)}) async-start(), calls=%async_computation.3 | async-start | bytes 3932160 | tf_op jit(solution)/shard_map/all_gather | solution.py:79
  8.0 133.5 %all-gather.4.cloned.1.call-start = ((), (), s32[]{:S(2)}) async-start(), calls=%async_computation.2 | async-start | bytes 3932160 | tf_op jit(solution)/shard_map/all_gather | solution.py:84
  8.7 455.6 %all-gather.8.cloned.1.call-start = ((), (), s32[]{:S(2)}) async-start(), calls=%async_computation.4 | async-start | bytes 23592960 | tf_op jit(solution)/shard_map/all_gather | solution.py:74
  9.4 26.8 %copy-start.13 = (bf16[1,8,1536]{2,1,0:T(8,128)(2,1)S(1)}, bf16[1,8,1536]{2,1,0:T(8,128)(2,1)}, u32[]{:S(2)}) copy-start(bf16[1,8,1536]{2,1,0:T(8,128)(2,1)} %param.18) | copy-start | bytes 73732
  9.4 515.2 %reduce-scatter.5.cloned.1.call-start = ((), (), s32[]{:S(2)}) async-start(), calls=%async_computation.6 | async-start | bytes 221184 | tf_op jit(solution)/shard_map/reduce_scatter | solution.py:186
  32.4 48.6 %copy-start.2 = (f32[256,64]{0,1:T(8,128)}, f32[256,64]{0,1:T(8,128)S(1)}, u32[]{:S(2)}) copy-start(f32[256,64]{0,1:T(8,128)S(1)} %get-tuple-element.28) | copy-start | bytes 196612
  32.4 48.6 %copy-start.6 = (f32[256,64]{0,1:T(8,128)}, f32[256,64]{0,1:T(8,128)S(1)}, u32[]{:S(2)}) copy-start(f32[256,64]{0,1:T(8,128)S(1)} %get-tuple-element.27) | copy-start | bytes 196612
  50.9 0.6 copy-start.10
  483.8 2.6 copy-start.9
  486.3 2.7 copy-start.5
  486.4 2.7 copy-start.8
  489.1 2.7 copy-start.17
  489.1 2.6 copy-start.4
  491.7 1.4 copy-start.3
  491.7 1.4 copy-start.7
  493.1 2.3 copy-start.11
  493.4 0.9 copy-start.1
  495.4 60.9 %reduce-scatter.3.cloned.1.call-start = ((), (), s32[]{:S(2)}) async-start(), calls=%async_computation.5 | async-start | bytes 442368 | tf_op jit(solution)/shard_map/reduce_scatter | solution.py:185
Sparse Core Ops, SparseCore 0:
  9.6 68.1 all-gather.5
  79.4 61.9 all-gather.3
  143.0 321.2 all-gather.7
  495.5 29.1 reduce-scatter.4
  527.4 28.8 reduce-scatter.2
where the time goes:
time: 563 us
  waiting for transfers between devices  444 us (79%)
  blocking collectives  45 us (8%)
  matrix products  32.2 us (6%)
  local copies, waits for them, and re-layouts  18 us (3%)
  between operations  14.1 us (3%)
  other arithmetic  8.88 us (2%)
    all_gather x1, waiting for transfers between devices, shards(): lax.all_gather(query_weight, 'dp', axis=0, tiled=True)  317 us
    all_gather x1, waiting for transfers between devices, shards(): lax.all_gather(value_weight, 'dp', axis=0, tiled=True)  54.4 us
    reduce_scatter x1, waiting for transfers between devices, shards(): lax.psum_scatter(down_term, ('dp', 'seq'), scatter_dimension=0, tiled=True)  31.6 us
    all_gather x1, waiting for transfers between devices, shards(): lax.all_gather(key_weight, 'dp', axis=0, tiled=True)  23.9 us
    all_gather x1, blocking collectives, shards(): lax.all_gather(adapter_down_weight, 'dp', axis=0, tiled=True)  15.9 us
    reduce_scatter x1, waiting for transfers between devices, shards(): lax.psum_scatter(up_term, ('dp', 'seq'), scatter_dimension=0, tiled=True)  15.1 us
    all_gather x1, blocking collectives, shards(): lax.all_gather(adapter_up_weight, 'dp', axis=0, tiled=True)  14.6 us
  transfers between devices with their start and end apart: 5, of which 5 were waited for; matrix products, arithmetic and copies ran while one was open for 5% of the time, Pallas kernels for 0%

commit v1 on v0

--- a/solution.py
+++ b/solution.py
@@ -1,9 +1,14 @@
+import functools
 import math
 
 import jax
 import jax.numpy as jnp
 from jax import lax
+from jax.experimental import pallas as pl
+from jax.experimental.pallas import tpu as pltpu
 from jax.sharding import PartitionSpec as P
+
+MESH = pl.DeviceIdType.MESH
 
 HEAD_SIZE = 128
 
@@ -30,6 +35,255 @@
 
 def doc_number(token_positions, doc_ends):
     return jnp.sum((token_positions[:, None] >= doc_ends[None, :]).astype(jnp.int32), axis=1)
+
+
+def project_kernel(
+    n, chunks, presplit,
+    x_ref, wq_ref, wk_ref, wv_ref, out_ref,
+    held, xs, load_sem, x_sem,
+    up_send, down_send, y_send, core_send, z_recv, y_recv, core_recv,
+):
+    depth = wq_ref.shape[0]
+    piece = depth // 4
+    rows = piece // chunks
+    g = lax.axis_index("groups")
+    z = lax.axis_index("dp")
+    s = lax.axis_index("seq")
+    above = n - 1 - z
+    below = z
+    both = jnp.minimum(above, below)
+
+    copies = []
+    at = 0
+    for i, ref in enumerate((wq_ref, wk_ref, wv_ref)):
+        width = ref.shape[1]
+        copies.append(
+            pltpu.make_async_copy(ref, held.at[z, :, pl.ds(at, width)], load_sem.at[i])
+        )
+        at += width
+    x_copies = []
+    for d in range(n):
+        src = x_ref.at[d] if presplit else x_ref.at[:, pl.ds(d * depth, depth)]
+        x_copies.append(pltpu.make_async_copy(src, xs.at[d], x_sem.at[d]))
+    for c in copies + x_copies:
+        c.start()
+
+    barrier = pltpu.get_barrier_semaphore()
+    pl.semaphore_signal(barrier, inc=1, device_id={"groups": 1 - g}, device_id_type=MESH)
+    pl.semaphore_signal(barrier, inc=1, device_id={"seq": 1 - s}, device_id_type=MESH)
+
+    @pl.when(z > 0)
+    def _():
+        pl.semaphore_signal(barrier, inc=1, device_id={"dp": z - 1}, device_id_type=MESH)
+
+    @pl.when(z < n - 1)
+    def _():
+        pl.semaphore_signal(barrier, inc=1, device_id={"dp": z + 1}, device_id_type=MESH)
+
+    pl.semaphore_wait(barrier, 2 + jnp.where(z > 0, 1, 0) + jnp.where(z < n - 1, 1, 0))
+
+    for c in copies:
+        c.wait()
+
+    def part(d, gg, ss, c):
+        start = pl.multiple_of(((gg * 2 + ss) * chunks + c) * rows, 16)
+        return held.at[d, pl.ds(start, rows), :]
+
+    def move(d, gg, ss, c, send, recv, target):
+        ref = part(d, gg, ss, c)
+        return pltpu.make_async_remote_copy(
+            src_ref=ref, dst_ref=ref, send_sem=send, recv_sem=recv,
+            device_id=target, device_id_type=MESH,
+        )
+
+    def to_below(d, c):
+        return move(d, g, s, c, down_send.at[d, c], z_recv.at[d, c], {"dp": jnp.maximum(z - 1, 0)})
+
+    def to_above(d, c):
+        return move(d, g, s, c, up_send.at[d, c], z_recv.at[d, c], {"dp": jnp.minimum(z + 1, n - 1)})
+
+    def to_group(d, c):
+        return move(d, g, s, c, y_send.at[d, c], y_recv.at[d, c], {"groups": 1 - g})
+
+    def from_group(d, c):
+        return move(d, 1 - g, s, c, y_send.at[d, c], y_recv.at[d, c], {"groups": 1 - g})
+
+    def to_core(d, gg, c, k):
+        return move(d, gg, s, c, core_send.at[d, c, k], core_recv.at[d, c, k], {"seq": 1 - s})
+
+    def from_core(d, gg, c, k):
+        return move(d, gg, 1 - s, c, core_send.at[d, c, k], core_recv.at[d, c, k], {"seq": 1 - s})
+
+    def send_own(c):
+        @pl.when(z > 0)
+        def _():
+            to_below(z, c).start()
+
+        @pl.when(z < n - 1)
+        def _():
+            to_above(z, c).start()
+
+    ahead = min(2, chunks)
+    for c in range(ahead):
+        send_own(c)
+    for c in x_copies:
+        c.wait()
+
+    tile = 512
+    tiles = out_ref.shape[1] // tile
+
+    def multiply(d, first):
+        def body(j, _):
+            cols = pl.ds(pl.multiple_of(j * tile, tile), tile)
+            term = jnp.dot(xs[d], held[d, :, cols], preferred_element_type=jnp.float32)
+            if first:
+                out_ref[:, cols] = term
+            else:
+                out_ref[:, cols] += term
+            return 0
+
+        lax.fori_loop(0, tiles, body, 0)
+
+    multiply(z, True)
+
+    def shard_of(k):
+        paired = k < 2 * both
+        half = k // 2
+        single = jnp.where(above > below, z + 1 + (k - both), z - 1 - (k - both))
+        return jnp.where(paired, jnp.where(k % 2 == 0, z + 1 + half, z - 1 - half), single)
+
+    def event(i):
+        paired = i < 2 * both * chunks
+        t = i // 2
+        t2 = i - both * chunks
+        up = jnp.where(paired, i % 2 == 0, above > below)
+        t = jnp.where(paired, t, t2)
+        return jnp.where(up, z + 1 + t // chunks, z - 1 - t // chunks), t % chunks
+
+    def land(d, c, onward, more):
+        to_below(d, c).wait_recv()
+
+        @pl.when(more)
+        def _():
+            onward(d, c).start()
+
+        to_group(d, c).start()
+        to_core(d, g, c, 0).start()
+
+    lag = min(2, chunks - 1)
+
+    def step(t, _):
+        @pl.when(t + ahead < chunks)
+        def _():
+            send_own(jnp.minimum(t + ahead, chunks - 1))
+
+        @pl.when(t < above * chunks)
+        def _():
+            land(jnp.minimum(z + 1 + t // chunks, n - 1), t % chunks, to_below, z > 0)
+
+        @pl.when(t < below * chunks)
+        def _():
+            land(jnp.maximum(z - 1 - t // chunks, 0), t % chunks, to_above, z < n - 1)
+
+        @pl.when(t >= lag)
+        def _():
+            cross(t - lag)
+
+        return 0
+
+    def cross(i):
+        d, c = event(i)
+        from_group(d, c).wait_recv()
+        to_core(d, 1 - g, c, 1).start()
+
+    def finish(k):
+        d = shard_of(k)
+
+        def body(c, _):
+            from_core(d, g, c, 0).wait_recv()
+            from_core(d, 1 - g, c, 1).wait_recv()
+            return 0
+
+        lax.fori_loop(0, chunks, body, 0)
+        multiply(d, False)
+
+    def phase(p, _):
+        lax.fori_loop(p * chunks, (p + 1) * chunks, step, 0)
+
+        @pl.when(p >= 2)
+        def _():
+            finish(jnp.maximum(p - 2, 0))
+
+        return 0
+
+    total = (n - 1) * chunks
+    lax.fori_loop(0, n - 1, phase, 0)
+    lax.fori_loop(total - lag, total, lambda i, _: (cross(i), 0)[1], 0)
+    for k in range(max(n - 3, 0), n - 1):
+        finish(jnp.int32(k))
+
+    def drain(i, _):
+        d = i // chunks
+        c = i % chunks
+        mine = d == z
+
+        @pl.when(jnp.logical_and(d >= z, z > 0))
+        def _():
+            to_below(d, c).wait_send()
+
+        @pl.when(jnp.logical_and(d <= z, z < n - 1))
+        def _():
+            to_above(d, c).wait_send()
+
+        @pl.when(jnp.logical_not(mine))
+        def _():
+            to_group(d, c).wait_send()
+            to_core(d, g, c, 0).wait_send()
+            to_core(d, 1 - g, c, 1).wait_send()
+
+        return 0
+
+    lax.fori_loop(0, n * chunks, drain, 0)
+
+
+def project(tokens, query_weight, key_weight, value_weight):
+    n = lax.axis_size("dp")
+    row_count = tokens.shape[0]
+    depth = query_weight.shape[0]
+    cols = query_weight.shape[1] + key_weight.shape[1] + value_weight.shape[1]
+    piece = depth // 4
+    chunks = max(c for c in range(1, 9) if piece % c == 0 and (piece // c) % 16 == 0)
+    presplit = depth % 128 != 0
+    if presplit:
+        tokens = jnp.transpose(tokens.reshape(row_count, n, depth), (1, 0, 2))
+    dma = pltpu.SemaphoreType.DMA
+    return pl.pallas_call(
+        functools.partial(project_kernel, n, chunks, presplit),
+        out_shape=jax.ShapeDtypeStruct((row_count, cols), jnp.float32),
+        in_specs=[pl.BlockSpec(memory_space=pl.ANY)] * 4,
+        out_specs=pl.BlockSpec(memory_space=pltpu.VMEM),
+        scratch_shapes=[
+            pltpu.VMEM((n, depth, cols), jnp.bfloat16),
+            pltpu.VMEM((n, row_count, depth), jnp.bfloat16),
+            dma((3,)),
+            dma((n,)),
+            dma((n, chunks)),
+            dma((n, chunks)),
+            dma((n, chunks)),
+            dma((n, chunks, 2)),
+            dma((n, chunks)),
+            dma((n, chunks)),
+            dma((n, chunks, 2)),
+        ],
+        compiler_params=pltpu.CompilerParams(
+            collective_id=0, has_side_effects=True, vmem_limit_bytes=50 * 2**20
+        ),
+        cost_estimate=pl.CostEstimate(
+            flops=2 * row_count * n * depth * cols,
+            bytes_accessed=2 * n * depth * cols,
+            transcendentals=0,
+        ),
+    )(tokens, query_weight, key_weight, value_weight)
 
 
 def shards(
@@ -69,35 +323,21 @@
         axis=1,
     )
     chooser = (stored_row[:, None] == adapter_ids[None, :]).astype(jnp.float32)
-    base_query = jnp.dot(
-        tokens,
-        lax.all_gather(query_weight, "dp", axis=0, tiled=True),
-        preferred_element_type=jnp.float32,
-    )
-    base_key = jnp.dot(
-        tokens,
-        lax.all_gather(key_weight, "dp", axis=0, tiled=True),
-        preferred_element_type=jnp.float32,
-    )
-    base_value = jnp.dot(
-        tokens,
-        lax.all_gather(value_weight, "dp", axis=0, tiled=True),
-        preferred_element_type=jnp.float32,
-    )
-    stored = (
-        lax.all_gather(adapter_down_weight, "dp", axis=0, tiled=True),
-        lax.all_gather(adapter_up_weight, "dp", axis=0, tiled=True),
-    )
+    projected = project(tokens, query_weight, key_weight, value_weight)
+    base_query = projected[:, :query_cols]
+    base_key = projected[:, query_cols : query_cols + key_cols]
+    base_value = projected[:, query_cols + key_cols :]
+    down_rows = lax.all_gather(jnp.transpose(adapter_down_weight[0]), ("dp", "owner"))
+    down_rows = jnp.transpose(
+        down_rows.reshape(adapters, -1, adapter_rank_size, quarter_part), (0, 2, 1, 3)
+    ).reshape(adapters * adapter_rank_size, tokens.shape[1])
+    stored = (None, lax.all_gather(adapter_up_weight, "dp", axis=0, tiled=True))
     up_weight_flat = stored[1].reshape(adapters * adapter_rank_size, query_cols)
     token_quarter = lax.dynamic_slice_in_dim(tokens, owner_at * quarter_part, quarter_part, 1)
-    down_weight_flat = jnp.transpose(stored[0], (1, 0, 2)).reshape(
-        quarter_part, adapters * adapter_rank_size
-    )
-    every_low = jnp.dot(
-        token_quarter, down_weight_flat, preferred_element_type=jnp.float32
+    every_low = lax.dot_general(
+        tokens, down_rows, (((1,), (1,)), ((), ())), preferred_element_type=jnp.float32
     ).reshape(row_count, adapters, adapter_rank_size)
-    partial_low = jnp.sum(every_low * chooser[:, :, None], axis=1)
-    low_rank = lax.psum(partial_low, "owner").astype(jnp.bfloat16)
+    low_rank = jnp.sum(every_low * chooser[:, :, None], axis=1).astype(jnp.bfloat16)
     spread = (
         (low_rank.astype(jnp.float32)[:, None, :] * chooser[:, :, None])
         .astype(jnp.bfloat16)

time: 563 us -> 292 us (0.52)
  waiting for transfers between devices: 444 us -> 48.8 us
  Pallas kernels: 0 us -> 142 us
  matrix products: 32.2 us -> 15.2 us
  blocking collectives: 45 us -> 53.9 us
  local copies, waits for them, and re-layouts: 18 us -> 10.3 us
    all_gather x3 -> x0, waiting for transfers between devices: 396 us -> none  [the longest x1 317 us: shards(): lax.all_gather(query_weight, 'dp', axis=0, tiled=True)]
    pallas_call x0 -> x1, Pallas kernels: none -> 142 us  [project(): pl.pallas_call(functools.partial(project_kernel, n, chunks, presplit), ou...]
    dot_general x4 -> x1, matrix products: 17.8 us -> 2.91 us  [shards(): lax.dot_general(tokens, down_rows, (((1,), (1,)), ((), ())), preferred_el...]
    all_gather x2, blocking collectives: 30.5 us -> 44.7 us  [the longest x1 31.2 us: shards(): lax.all_gather(jnp.transpose(adapter_down_weight[0]), ('dp', 'owner'))]
  transfers between devices with their start and end apart: 5 -> 2, of which waited for: 5 -> 2; matrix products, arithmetic and copies ran while one was open for 5% -> 3% of each run, Pallas kernels for 0% -> 0%
where the time goes in v1:
time: 292 us
  Pallas kernels  142 us (49%)
  blocking collectives  53.9 us (18%)
  waiting for transfers between devices  48.8 us (17%)
  matrix products  15.2 us (5%)
  between operations  14.3 us (5%)
  local copies, waits for them, and re-layouts  10.3 us (4%)
  other arithmetic  6.93 us (2%)
    pallas_call x1, Pallas kernels, project(): pl.pallas_call(functools.partial(project_kernel, n, chunks, presplit), ou...  142 us
    reduce_scatter x1, waiting for transfers between devices, shards(): lax.psum_scatter(down_term, ('dp', 'seq'), scatter_dimension=0, tiled=True)  31.8 us
    all_gather x1, blocking collectives, shards(): lax.all_gather(jnp.transpose(adapter_down_weight[0]), ('dp', 'owner'))  31.2 us
    reduce_scatter x1, waiting for transfers between devices, shards(): lax.psum_scatter(up_term, ('dp', 'seq'), scatter_dimension=0, tiled=True)  17 us
    all_gather x1, blocking collectives, shards(): stored = (None, lax.all_gather(adapter_up_weight, 'dp', axis=0, tiled=True))  13.6 us
  transfers between devices with their start and end apart: 2, of which 2 were waited for; matrix products, arithmetic and copies ran while one was open for 3% of the time, Pallas kernels for 0%

profile of v1, /device:TPU:0, one launch (start us, length us, event | category | flops | bytes accessed | tf_op | source)
XLA Modules:
  0.0 291.6 jit_solution(15579509152081136475)
XLA Ops:
  7.3 1.1 copy-done
  8.4 1.1 copy-done.1
  9.5 142.1 %shard_map.121 = f32[256,2048]{1,0:T(8,128)S(1)} custom-call(bf16[256,6144]{1,0:T(8,128)(2,1)} %x_ref.1, bf16[1536,1536]{1,0:T(8,128)(2,1)} %wq_ref.1, bf16[1536,256]{1,0:T(8,128)(2,1)S(1)} %copy-done, bf16[1536,256]{1,0:T(8,128)(2,1)S(1)} %copy-done.1), custom_call_target="tpu_custom_call" | custom-call | flops 6442450944 | bytes 25165824 | tf_op jit(solution)/shard_map/pallas_call | solution.py:260
  151.7 0.7 slice.54
  152.4 0.9 broadcast_multiply_fusion
  153.6 0.3 fusion.59
  154.2 2.0 all_gather.16
  156.3 0.7 convert_reduce_fusion
  157.3 31.2 %all-gather = bf16[64,3072]{1,0:T(8,128)(2,1)S(1)} all-gather(bf16[8,3072]{1,0:T(8,128)(2,1)S(1)} %bitcast.132), channel_id=2, replica_groups=mesh['groups'=2,'dp'=4,'owner'=2,'seq'=2] {'dp','owner'}, dimensions={0}, use_global_device_ids=true | all-gather | bytes 442368 | tf_op jit(solution)/shard_map/all_gather | solution.py:330
  188.5 2.9 fusion.28
  191.4 13.6 %all_gather.19 = bf16[4,8,1536]{2,1,0:T(8,128)(2,1)S(1)} all-gather(bf16[1,8,1536]{2,1,0:T(8,128)(2,1)} %param.18), channel_id=1, replica_groups=mesh['groups'=2,'dp'=4,'owner'=2,'seq'=2] {'dp'}, dimensions={0}, use_global_device_ids=true | all-gather | bytes 122880 | tf_op jit(solution)/shard_map/all_gather | solution.py:334
  205.0 1.6 fusion.15
  206.5 1.9 copy.83
  208.7 0.4 copy.84
  209.0 0.4 copy.85
  209.4 1.5 fusion.36
  210.9 1.0 copy.103
  211.9 2.1 all_gather.15
  214.0 0.3 copy.87
  214.3 1.1 fusion.32
  215.4 2.7 fusion.60
  218.1 1.1 fusion.1
  219.2 1.6 copy-done.13
  220.8 1.4 fusion.19
  222.5 1.0 fusion.43
  223.6 0.2 fusion.31
  223.8 5.0 %psum.7 = bf16[256,8]{0,1:T(8,128)(2,1)S(1)} all-reduce(f32[256,8]{0,1:T(8,128)S(1)} %fusion.31), channel_id=1, replica_groups=mesh['groups'=2,'dp'=4,'owner'=2,'seq'=2] {'owner'}, use_global_device_ids=true, to_apply=%region_10.11 | all-reduce | flops 2048 | bytes 12288 | tf_op jit(solution)/shard_map/psum | solution.py:401
  228.8 2.6 fusion.16
  231.4 3.4 %fusion.22 = bf16[2,128,6,256]{3,1,2,0:T(8,128)(2,1)S(1)} fusion(bf16[512,2,128]{0,2,1:T(8,128)(2,1)S(1)} %copy-done.6, f32[2,6,256,512]{2,3,1,0:T(8,128)} %copy-done.13, f32[2,6,256]{2,1,0:T(8,128)S(1)} %get-tuple-element.29), kind=kOutput, calls=%fused_computation.25 | convolution fusion | flops 406192128 | bytes 7352320 | tf_op jit(solution)/shard_map/cgqk,kcd->qcgd/dot_general | solution.py:378
  234.8 1.2 copy.93
  236.0 17.0 %reduce-scatter.5.cloned.1.call-done = f32[1,8,768]{2,1,0:T(8,128)} async-done(((f32[8,8,768]{2,1,0:T(8,128)}), f32[1,8,768]{2,1,0:T(8,128)}) %reduce-scatter.5.cloned.1.call-update) | async-done | bytes 24592 | tf_op jit(solution)/shard_map/reduce_scatter | solution.py:426
  252.9 31.8 %reduce-scatter.3.cloned.1.call-done = f32[1,1536,8]{1,2,0:T(8,128)} async-done(((f32[8,1536,8]{1,2,0:T(8,128)}), f32[1,1536,8]{1,2,0:T(8,128)}) %reduce-scatter.3.cloned.1.call-update) | async-done | bytes 49168 | tf_op jit(solution)/shard_map/reduce_scatter | solution.py:425
  (48 shorter events, 1.7 us)
Async XLA Ops:
  7.2 245.8 %reduce-scatter.5.cloned.1.call-start = ((), (), s32[]{:S(2)}) async-start(), calls=%async_computation.3 | async-start | bytes 221184 | tf_op jit(solution)/shard_map/reduce_scatter | solution.py:426
  7.3 1.1 copy-start
  8.4 1.1 copy-start.1
  9.5 147.5 %copy-start.9 = (s32[256]{0:T(256)}, s32[256]{0:T(256)S(1)}, u32[]{:S(2)}) copy-start(s32[256]{0:T(256)S(1)} %iota_add_fusion) | copy-start | bytes 3076
  9.5 146.6 %copy-start.12 = (s32[1,4]{1,0:T(1,128)S(1)}, s32[1,4]{1,0:T(1,128)}, u32[]{:S(2)}) copy-start(s32[1,4]{1,0:T(1,128)} %param.11) | copy-start | bytes 52
  9.5 147.6 %copy-start.10 = (s32[1,4]{1,0:T(1,128)S(1)}, s32[1,4]{1,0:T(1,128)}, u32[]{:S(2)}) copy-start(s32[1,4]{1,0:T(1,128)} %param.12) | copy-start | bytes 52
  9.5 147.7 %copy-start.11 = (s32[4]{0:T(128)S(1)}, s32[4]{0:T(128)}, u32[]{:S(2)}) copy-start(s32[4]{0:T(128)} %param.13) | copy-start | bytes 52
  9.5 147.8 %copy-start.8 = (bf16[1,3072,8]{1,2,0:T(8,128)(2,1)S(1)}, bf16[1,3072,8]{1,2,0:T(8,128)(2,1)}, u32[]{:S(2)}) copy-start(bf16[1,3072,8]{1,2,0:T(8,128)(2,1)} %param.17) | copy-start | bytes 147460
  191.4 22.7 %copy-start.2 = (bf16[256,1536]{1,0:T(8,128)(2,1)S(1)}, bf16[256,1536]{1,0:T(8,128)(2,1)}, u32[]{:S(2)}) copy-start(bf16[256,1536]{1,0:T(8,128)(2,1)} %param.19) | copy-start | bytes 2359300
  205.0 3.4 %copy-start.3 = (bf16[4,8,1536]{2,1,0:T(8,128)(2,1)}, bf16[4,8,1536]{2,1,0:T(8,128)(2,1)S(1)}, u32[]{:S(2)}) copy-start(bf16[4,8,1536]{2,1,0:T(8,128)(2,1)S(1)} %all_gather.19) | copy-start | bytes 294916
  214.3 1.1 copy-start.7
  215.4 2.7 copy-start.6
  218.1 2.7 copy-start.13
  220.8 1.4 copy-start.5
  220.8 2.8 copy-start.4
  223.5 61.2 %reduce-scatter.3.cloned.1.call-start = ((), (), s32[]{:S(2)}) async-start(), calls=%async_computation.2 | async-start | bytes 442368 | tf_op jit(solution)/shard_map/reduce_scatter | solution.py:425
Sparse Core Ops, SparseCore 0:
  223.6 29.2 reduce-scatter.4
  255.9 28.8 reduce-scatter.2

commit v2 on v1

v2 whole, which is shorter than its diff:
```python
import functools
import math

import jax
import jax.numpy as jnp
from jax import lax
from jax.experimental import pallas as pl
from jax.experimental.pallas import tpu as pltpu
from jax.sharding import PartitionSpec as P

MESH = pl.DeviceIdType.MESH

HEAD_SIZE = 128


rope_base = 1000000.0
neg_big = -1e30


def doc_number(token_positions, doc_ends):
    return jnp.sum((token_positions[:, None] >= doc_ends[None, :]).astype(jnp.int32), axis=1)


def whole_kernel(
    n, owners, chunks, presplit,
    x_ref, xq_ref, wq_ref, wk_ref, wv_ref, pack_ref, cot_ref,
    cos_ref, sin_ref, start_ref, choose_ref,
    att_ref, down_ref, up_ref,
    out_ref, held, xs, xq, packs, cot, ups, spread, low, mid, kv, bias, gq,
    give, got, keep, gath,
    load_sem, x_sem,
    up_send, down_send, y_send, core_send, z_recv, y_recv, core_recv,
    pack_send, pack_recv, low_send, low_recv, mid_send, mid_recv,
    kv_sem, got_sem, gath_send, gath_recv,
):
    depth = wq_ref.shape[0]
    row_count = xq.shape[0]
    query_cols = wq_ref.shape[1]
    key_cols = wk_ref.shape[1]
    rank = low.shape[1]
    o = lax.axis_index("owner")
    piece = depth // 4
    rows = piece // chunks
    g = lax.axis_index("groups")
    z = lax.axis_index("dp")
    s = lax.axis_index("seq")
    above = n - 1 - z
    below = z
    both = jnp.minimum(above, below)

    copies = []
    at = 0
    for i, ref in enumerate((wq_ref, wk_ref, wv_ref)):
        width = ref.shape[1]
        copies.append(
            pltpu.make_async_copy(ref, held.at[z, :, pl.ds(at, width)], load_sem.at[i])
        )
        at += width
    x_copies = []
    for d in range(n):
        src = x_ref.at[d] if presplit else x_ref.at[:, pl.ds(d * depth, depth)]
        x_copies.append(pltpu.make_async_copy(src, xs.at[d], x_sem.at[d]))
    width = xq.shape[1]
    x_copies.append(
        pltpu.make_async_copy(
            xq_ref.at[:, pl.ds(pl.multiple_of(o * width, 128), width)], xq, load_sem.at[3]
        )
    )
    x_copies.append(pltpu.make_async_copy(cot_ref, cot, load_sem.at[4]))
    copies.append(pltpu.make_async_copy(pack_ref, packs.at[z], load_sem.at[5]))
    for c in copies + x_copies:
        c.start()

    barrier = pltpu.get_barrier_semaphore()
    pl.semaphore_signal(barrier, inc=1, device_id={"groups": 1 - g}, device_id_type=MESH)
    pl.semaphore_signal(barrier, inc=1, device_id={"seq": 1 - s}, device_id_type=MESH)
    for k in range(1, n):
        pl.semaphore_signal(
            barrier, inc=1, device_id={"dp": lax.rem(z + k, n)}, device_id_type=MESH
        )
    for k in range(1, owners):
        pl.semaphore_signal(
            barrier, inc=1, device_id={"owner": lax.rem(o + k, owners)}, device_id_type=MESH
        )
    pl.semaphore_wait(barrier, n + owners)

    for c in copies:
        c.wait()

    def part(d, gg, ss, c):
        start = pl.multiple_of(((gg * 2 + ss) * chunks + c) * rows, 16)
        return held.at[d, pl.ds(start, rows), :]

    def move(d, gg, ss, c, send, recv, target):
        ref = part(d, gg, ss, c)
        return pltpu.make_async_remote_copy(
            src_ref=ref, dst_ref=ref, send_sem=send, recv_sem=recv,
            device_id=target, device_id_type=MESH,
        )

    def to_below(d, c):
        return move(d, g, s, c, down_send.at[d, c], z_recv.at[d, c], {"dp": jnp.maximum(z - 1, 0)})

    def to_above(d, c):
        return move(d, g, s, c, up_send.at[d, c], z_recv.at[d, c], {"dp": jnp.minimum(z + 1, n - 1)})

    def to_group(d, c):
        return move(d, g, s, c, y_send.at[d, c], y_recv.at[d, c], {"groups": 1 - g})

    def from_group(d, c):
        return move(d, 1 - g, s, c, y_send.at[d, c], y_recv.at[d, c], {"groups": 1 - g})

    def to_core(d, gg, c, k):
        return move(d, gg, s, c, core_send.at[d, c, k], core_recv.at[d, c, k], {"seq": 1 - s})

    def from_core(d, gg, c, k):
        return move(d, gg, 1 - s, c, core_send.at[d, c, k], core_recv.at[d, c, k], {"seq": 1 - s})

    def send_own(c):
        @pl.when(z > 0)
        def _():
            to_below(z, c).start()

        @pl.when(z < n - 1)
        def _():
            to_above(z, c).start()

    ahead = min(2, chunks)
    for c in range(ahead):
        send_own(c)
    pack_copies = [
        pltpu.make_async_remote_copy(
            src_ref=packs.at[z], dst_ref=packs.at[z],
            send_sem=pack_send.at[k], recv_sem=pack_recv.at[k],
            device_id={"dp": lax.rem(z + k, n)}, device_id_type=MESH,
        )
        for k in range(1, n)
    ]
    for c in pack_copies:
        c.start()
    for c in x_copies:
        c.wait()

    kpos = lax.broadcasted_iota(jnp.int32, bias.shape, 1)
    qpos = s * row_count + lax.broadcasted_iota(jnp.int32, bias.shape, 0)
    allowed = jnp.logical_and(kpos <= qpos, kpos >= start_ref[:, :1])
    bias[...] = jnp.where(allowed, 0.0, neg_big)

    def owner_copies(buf, send, recv):
        return [
            pltpu.make_async_remote_copy(
                src_ref=buf.at[0], dst_ref=buf.at[k],
                send_sem=send.at[k], recv_sem=recv.at[k],
                device_id={"owner": lax.rem(o + k, owners)}, device_id_type=MESH,
            )
            for k in range(1, owners)
        ]

    def chosen(wide):
        return jnp.sum((wide * choose_ref[...]).reshape(n, rank, row_count), axis=0)

    def spread_out(buf):
        total = buf[0]
        for k in range(1, owners):
            total = total + buf[k]
        total = total.astype(jnp.bfloat16).astype(jnp.float32)
        return (jnp.concatenate([total] * n, axis=0) * choose_ref[...]).astype(jnp.bfloat16)

    low_copies = owner_copies(low, low_send, low_recv)
    mid_copies = owner_copies(mid, mid_send, mid_recv)

    def low_first():
        for c in pack_copies:
            c.wait_recv()
        wide = packs[...].astype(jnp.float32)
        ups[...] = wide[:, :rank, :query_cols].reshape(n * rank, query_cols).astype(jnp.bfloat16)
        downs = jnp.concatenate([wide[:, :rank, query_cols:], wide[:, rank:, :]], axis=2)
        downs = downs.reshape(n * rank, width).astype(jnp.bfloat16)
        low[0] = chosen(
            lax.dot_general(
                downs, xq[...], (((1,), (1,)), ((), ())), preferred_element_type=jnp.float32
            )
        )
        for c in low_copies:
            c.start()

    def low_second():
        for c in low_copies:
            c.wait_recv()
        spread[...] = spread_out(low)

        def body(j, _):
            cols = pl.ds(pl.multiple_of(j * 256, 256), 256)
            out_ref[:, cols] += lax.dot_general(
                spread[...], ups[:, cols], (((0,), (0,)), ((), ())),
                preferred_element_type=jnp.float32,
            )
            return 0

        lax.fori_loop(0, query_cols // 256, body, 0)

    tile = 512
    tiles = out_ref.shape[1] // tile

    def multiply(d, first):
        def body(j, _):
            cols = pl.ds(pl.multiple_of(j * tile, tile), tile)
            term = jnp.dot(xs[d], held[d, :, cols], preferred_element_type=jnp.float32)
            if first:
                out_ref[:, cols] = term
            else:
                out_ref[:, cols] += term
            return 0

        lax.fori_loop(0, tiles, body, 0)

    multiply(z, True)

    def shard_of(k):
        paired = k < 2 * both
        half = k // 2
        single = jnp.where(above > below, z + 1 + (k - both), z - 1 - (k - both))
        return jnp.where(paired, jnp.where(k % 2 == 0, z + 1 + half, z - 1 - half), single)

    def event(i):
        paired = i < 2 * both * chunks
        t = i // 2
        t2 = i - both * chunks
        up = jnp.where(paired, i % 2 == 0, above > below)
        t = jnp.where(paired, t, t2)
        return jnp.where(up, z + 1 + t // chunks, z - 1 - t // chunks), t % chunks

    def land(d, c, onward, more):
        to_below(d, c).wait_recv()

        @pl.when(more)
        def _():
            onward(d, c).start()

        to_group(d, c).start()
        to_core(d, g, c, 0).start()

    lag = min(2, chunks - 1)

    def step(t, _):
        @pl.when(t + ahead < chunks)
        def _():
            send_own(jnp.minimum(t + ahead, chunks - 1))

        @pl.when(t < above * chunks)
        def _():
            land(jnp.minimum(z + 1 + t // chunks, n - 1), t % chunks, to_below, z > 0)

        @pl.when(t < below * chunks)
        def _():
            land(jnp.maximum(z - 1 - t // chunks, 0), t % chunks, to_above, z < n - 1)

        @pl.when(t >= lag)
        def _():
            cross(t - lag)

        return 0

    def cross(i):
        d, c = event(i)
        from_group(d, c).wait_recv()
        to_core(d, 1 - g, c, 1).start()

    def finish(k):
        d = shard_of(k)

        def body(c, _):
            from_core(d, g, c, 0).wait_recv()
            from_core(d, 1 - g, c, 1).wait_recv()
            return 0

        lax.fori_loop(0, chunks, body, 0)
        multiply(d, False)

    def phase(p, _):
        lax.fori_loop(p * chunks, (p + 1) * chunks, step, 0)

        @pl.when(p == 0)
        def _():
            low_first()

        @pl.when(p >= 2)
        def _():
            finish(jnp.maximum(p - 2, 0))

        return 0

    total = (n - 1) * chunks
    lax.fori_loop(0, n - 1, phase, 0)
    lax.fori_loop(total - lag, total, lambda i, _: (cross(i), 0)[1], 0)
    low_second()
    for k in range(max(n - 3, 0), n - 1):
        finish(jnp.int32(k))

    half = HEAD_SIZE // 2

    def rotate(v, direction):
        turned = pltpu.roll(v, half, 1) * sin_ref[...]
        return v * cos_ref[...] + (turned if direction > 0 else -turned)

    for c in range(key_cols // HEAD_SIZE):
        cols = pl.ds(c * HEAD_SIZE, HEAD_SIZE)
        raw = out_ref[:, pl.ds(query_cols + c * HEAD_SIZE, HEAD_SIZE)]
        kv[s, :, cols] = rotate(raw, 1).astype(jnp.bfloat16)
    kv[s, :, pl.ds(key_cols, key_cols)] = out_ref[
        :, pl.ds(query_cols + key_cols, key_cols)
    ].astype(jnp.bfloat16)
    kv_copy = pltpu.make_async_remote_copy(
        src_ref=kv.at[s], dst_ref=kv.at[s], send_sem=kv_sem.at[0], recv_sem=kv_sem.at[1],
        device_id={"seq": 1 - s}, device_id_type=MESH,
    )
    kv_copy.start()
    pltpu.make_async_remote_copy(
        src_ref=kv.at[1 - s], dst_ref=kv.at[1 - s], send_sem=kv_sem.at[0],
        recv_sem=kv_sem.at[1], device_id={"seq": 1 - s}, device_id_type=MESH,
    ).wait_recv()

    scale = 1.0 / math.sqrt(HEAD_SIZE)
    grouping = query_cols // key_cols

    def dot(a, b, da, db):
        return lax.dot_general(
            a, b, (((da,), (db,)), ((), ())), preferred_element_type=jnp.float32
        )

    def head(j, _):
        cols = pl.ds(pl.multiple_of(j * HEAD_SIZE, HEAD_SIZE), HEAD_SIZE)
        at = pl.multiple_of((j // grouping) * HEAD_SIZE, HEAD_SIZE)
        keys = kv[:, :, pl.ds(at, HEAD_SIZE)].reshape(2 * row_count, HEAD_SIZE)
        values = kv[:, :, pl.ds(at + key_cols, HEAD_SIZE)].reshape(2 * row_count, HEAD_SIZE)
        query = rotate(out_ref[:, cols], 1).astype(jnp.bfloat16)
        scores = dot(query, keys, 1, 1) * scale + bias[...]
        raised = jnp.exp(scores - jnp.max(scores, axis=1, keepdims=True))
        probability = raised * (1.0 / jnp.sum(raised, axis=1, keepdims=True))
        att_ref[:, cols] = dot(probability.astype(jnp.bfloat16), values, 1, 0).astype(
            jnp.bfloat16
        )
        dprob = dot(cot[:, cols], values, 1, 1)
        delta = jnp.sum(probability * dprob, axis=1, keepdims=True)
        dscore = (probability * (dprob - delta)).astype(jnp.bfloat16)
        gq[:, cols] = rotate(dot(dscore, keys, 1, 0) * scale, -1).astype(jnp.bfloat16)
        return 0

    lax.fori_loop(0, query_cols // HEAD_SIZE, head, 0)

    mid[0] = chosen(dot(ups[...], gq[...], 1, 1))
    for c in mid_copies:
        c.start()
    down_half = width // 2
    up_half = query_cols // 2

    def up_term(h):
        return dot(spread[...], gq[:, pl.ds(pl.multiple_of(h * up_half, 128), up_half)], 1, 0)

    def down_term(m, h):
        return dot(m, xq[:, pl.ds(pl.multiple_of(h * down_half, 128), down_half)], 1, 0)

    give[:, pl.ds(down_half, up_half)] = up_term(1 - s)
    for c in mid_copies:
        c.wait_recv()
    spread_mid = spread_out(mid)
    give[:, pl.ds(0, down_half)] = down_term(spread_mid, 1 - s)
    swap = pltpu.make_async_remote_copy(
        src_ref=give, dst_ref=got, send_sem=got_sem.at[0], recv_sem=got_sem.at[1],
        device_id={"seq": 1 - s}, device_id_type=MESH,
    )
    swap.start()
    mine_up = up_term(s)
    mine_down = down_term(spread_mid, s)
    swap.wait_recv()
    keep[:, :, pl.ds(0, down_half)] = (mine_down + got[:, pl.ds(0, down_half)]).reshape(
        n, rank, down_half
    )
    keep[:, :, pl.ds(down_half, up_half)] = (
        mine_up + got[:, pl.ds(down_half, up_half)]
    ).reshape(n, rank, up_half)
    gath_copies = [
        pltpu.make_async_remote_copy(
            src_ref=keep.at[lax.rem(z + k, n)], dst_ref=gath.at[k],
            send_sem=gath_send.at[k], recv_sem=gath_recv.at[k],
            device_id={"dp": lax.rem(z + k, n)}, device_id_type=MESH,
        )
        for k in range(1, n)
    ]
    for c in gath_copies:
        c.start()
    total_grad = keep[z]
    for k, c in enumerate(gath_copies):
        c.wait_recv()
        total_grad = total_grad + gath[k + 1]
    down_ref[...] = total_grad[:, :down_half]
    up_ref[...] = total_grad[:, down_half:]

    for c in pack_copies + low_copies + mid_copies + gath_copies + [kv_copy, swap]:
        c.wait_send()

    def drain(i, _):
        d = i // chunks
        c = i % chunks
        mine = d == z

        @pl.when(jnp.logical_and(d >= z, z > 0))
        def _():
            to_below(d, c).wait_send()

        @pl.when(jnp.logical_and(d <= z, z < n - 1))
        def _():
            to_above(d, c).wait_send()

        @pl.when(jnp.logical_not(mine))
        def _():
            to_group(d, c).wait_send()
            to_core(d, g, c, 0).wait_send()
            to_core(d, 1 - g, c, 1).wait_send()

        return 0

    lax.fori_loop(0, n * chunks, drain, 0)


def whole(
    tokens, query_weight, key_weight, value_weight, pack, cotangent, cosines, sines, starts, choose
):
    n = lax.axis_size("dp")
    owners = lax.axis_size("owner")
    row_count, width = tokens.shape
    depth, query_cols = query_weight.shape
    key_cols = key_weight.shape[1]
    cols = query_cols + 2 * key_cols
    wide = choose.shape[0]
    rank = wide // n
    quarter = width // owners
    summed = (quarter + query_cols) // 2
    piece = depth // 4
    chunks = max(c for c in range(1, 9) if piece % c == 0 and (piece // c) % 16 == 0)
    presplit = depth % 128 != 0
    split = tokens
    if presplit:
        split = jnp.transpose(tokens.reshape(row_count, n, depth), (1, 0, 2))
    dma = pltpu.SemaphoreType.DMA
    bf16 = jnp.bfloat16
    f32 = jnp.float32
    return pl.pallas_call(
        functools.partial(whole_kernel, n, owners, chunks, presplit),
        out_shape=(
            jax.ShapeDtypeStruct((row_count, query_cols), bf16),
            jax.ShapeDtypeStruct((rank, quarter // 2), f32),
            jax.ShapeDtypeStruct((rank, query_cols // 2), f32),
        ),
        in_specs=[pl.BlockSpec(memory_space=pl.ANY)] * 7
        + [pl.BlockSpec(memory_space=pltpu.VMEM)] * 4,
        out_specs=(pl.BlockSpec(memory_space=pltpu.VMEM),) * 3,
        scratch_shapes=[
            pltpu.VMEM((row_count, cols), f32),
            pltpu.VMEM((n, depth, cols), bf16),
            pltpu.VMEM((n, row_count, depth), bf16),
            pltpu.VMEM((row_count, quarter), bf16),
            pltpu.VMEM((n,) + pack.shape, bf16),
            pltpu.VMEM((row_count, query_cols), bf16),
            pltpu.VMEM((wide, query_cols), bf16),
            pltpu.VMEM((wide, row_count), bf16),
            pltpu.VMEM((owners, rank, row_count), f32),
            pltpu.VMEM((owners, rank, row_count), f32),
            pltpu.VMEM((2, row_count, 2 * key_cols), bf16),
            pltpu.VMEM((row_count, 2 * row_count), f32),
            pltpu.VMEM((row_count, query_cols), bf16),
            pltpu.VMEM((wide, summed), f32),
            pltpu.VMEM((wide, summed), f32),
            pltpu.VMEM((n, rank, summed), f32),
            pltpu.VMEM((n, rank, summed), f32),
            dma((6,)),
            dma((n,)),
            dma((n, chunks)),
            dma((n, chunks)),
            dma((n, chunks)),
            dma((n, chunks, 2)),
            dma((n, chunks)),
            dma((n, chunks)),
            dma((n, chunks, 2)),
            dma((n,)),
            dma((n,)),
            dma((owners,)),
            dma((owners,)),
            dma((owners,)),
            dma((owners,)),
            dma((2,)),
            dma((2,)),
            dma((n,)),
            dma((n,)),
        ],
        compiler_params=pltpu.CompilerParams(
            collective_id=0, has_side_effects=True, vmem_limit_bytes=56 * 2**20
        ),
        cost_estimate=pl.CostEstimate(
            flops=2 * row_count * n * depth * cols,
            bytes_accessed=2 * n * depth * cols,
            transcendentals=0,
        ),
    )(
        split, tokens, query_weight, key_weight, value_weight, pack, cotangent,
        cosines, sines, starts, choose,
    )


def shards(
    tokens,
    document_lengths,
    document_adapter,
    adapter_stored_row,
    query_weight,
    key_weight,
    value_weight,
    adapter_down_weight,
    adapter_up_weight,
    output_cotangent,
):
    row_count = tokens.shape[0]
    rank = adapter_down_weight.shape[2]
    adapters = lax.axis_size("dp")
    doc_count = document_lengths.shape[1]
    doc_ends = jnp.cumsum(document_lengths[0])
    own_positions = lax.axis_index("seq") * row_count + jnp.arange(row_count, dtype=jnp.int32)
    doc_mine = doc_number(own_positions, doc_ends)
    in_document = doc_mine[:, None] == jnp.arange(doc_count, dtype=jnp.int32)[None, :]
    starts = jnp.sum(jnp.where(in_document, (doc_ends - document_lengths[0])[None, :], 0), axis=1)
    starts = jnp.broadcast_to(starts[:, None], (row_count, HEAD_SIZE))
    adapter_of = jnp.sum(jnp.where(in_document, document_adapter[0][None, :], 0), axis=1)
    adapter_ids = jnp.arange(adapters, dtype=jnp.int32)
    stored_row = jnp.sum(
        jnp.where(adapter_of[:, None] == adapter_ids[None, :], adapter_stored_row[None, :], 0),
        axis=1,
    )
    row_of = jnp.arange(adapters * rank, dtype=jnp.int32) // rank
    choose = (row_of[:, None] == stored_row[None, :]).astype(jnp.float32)
    half_width = HEAD_SIZE // 2
    frequency = rope_base ** (
        -(jnp.arange(half_width).astype(jnp.float32) * 2.0 / HEAD_SIZE)
    )
    angles = own_positions.astype(jnp.float32)[:, None] * frequency[None, :]
    cosines = jnp.cos(angles)
    sines = jnp.sin(angles)
    cosines = jnp.concatenate([cosines, cosines], axis=1)
    sines = jnp.concatenate([-sines, sines], axis=1)
    line = jnp.concatenate([adapter_up_weight[0], jnp.transpose(adapter_down_weight[0])], axis=1)
    middle = line.shape[1] // 2
    pack = jnp.concatenate([line[:, :middle], line[:, middle:]], axis=0)
    attended, grad_down, grad_up = whole(
        tokens, query_weight, key_weight, value_weight, pack, output_cotangent,
        cosines, sines, starts, choose,
    )
    return (attended, jnp.transpose(grad_down)[None], grad_up[None])


def solution(mesh):
    in_specs = (
        P(("groups", "dp", "seq"), None),
        P(("groups", "dp"), None),
        P(("groups", "dp"), None),
        P(),
        P("dp", "owner"),
        P("dp", "owner"),
        P("dp", "owner"),
        P("dp", "owner", None),
        P("dp", None, "owner"),
        P(("groups", "dp", "seq"), "owner"),
    )
    out_specs = (
        P(("groups", "dp", "seq"), "owner"),
        P(("groups", "dp"), ("owner", "seq"), None),
        P(("groups", "dp"), None, ("owner", "seq")),
    )
    return jax.shard_map(shards, mesh=mesh, in_specs=in_specs, out_specs=out_specs, check_vma=False)
```

time: 292 us -> 190 us (0.65)
  blocking collectives: 53.9 us -> 0 us
  waiting for transfers between devices: 48.8 us -> 0 us
  Pallas kernels: 142 us -> 175 us
  matrix products: 15.2 us -> 0 us
  between operations: 14.3 us -> 0.66 us
  local copies, waits for them, and re-layouts: 10.3 us -> 6.36 us
    all_gather x4 -> x0, blocking collectives: 48.9 us -> none  [the longest x1 31.2 us: shards(): lax.all_gather(jnp.transpose(adapter_down_weight[0]), ('dp', 'owner'))]
    reduce_scatter x2 -> x0, waiting for transfers between devices: 48.8 us -> none  [the longest x1 31.8 us: shards(): lax.psum_scatter(down_term, ('dp', 'seq'), scatter_dimension=0, tiled=True)]
    pallas_call x1, Pallas kernels: 142 us -> 175 us  [whole(): pl.pallas_call(functools.partial(whole_kernel, n, owners, chunks, prespli...]
    dot_general x9 -> x0, matrix products: 15.2 us -> none  [the longest x1 3.39 us: shards(): jnp.einsum('cgqk,kcd->qcgd', weights, values_seen, preferred_element_type...]
    psum x1 -> x0, blocking collectives: 5.02 us -> none  [shards(): mid_rank = lax.psum(partial_mid, 'owner').astype(jnp.bfloat16)]
  transfers between devices with their start and end apart: 2 -> 0, of which waited for: 2 -> 0; matrix products, arithmetic and copies ran while one was open for 3% -> 0% of each run, Pallas kernels for 0% -> 0%
where the time goes in v2:
time: 190 us; the launch traced here: 189 us
  Pallas kernels  175 us (92%)
  other arithmetic  7.21 us (4%)
  local copies, waits for them, and re-layouts  6.36 us (3%)
    pallas_call x1, Pallas kernels, whole(): pl.pallas_call(functools.partial(whole_kernel, n, owners, chunks, prespli...  175 us
    unnamed x3, local copies, waits for them, and re-layouts  4.83 us

profile of v2, /device:TPU:0, one launch (start us, length us, event | category | flops | bytes accessed | tf_op | source)
XLA Modules:
  0.0 189.4 jit_solution(10956297534679829770)
XLA Ops:
  0.6 0.8 reduce-window.4
  1.5 0.7 fusion.2
  2.1 0.1 convert_reduce_fusion
  2.2 0.7 select_reduce_fusion.1
  3.0 0.7 select_reduce_fusion
  3.7 0.7 compare_convert_fusion.choose_ref
  4.4 0.8 slice.8
  5.2 1.4 fusion.pack_ref
  6.6 0.8 broadcast_in_dim.55.start_ref
  7.3 0.5 fusion.1
  7.9 0.8 pad_maximum_fusion.1.sin_ref
  8.6 0.8 pad_maximum_fusion.cos_ref
  9.4 175.2 %shard_map.121 = (bf16[256,1536]{1,0:T(8,128)(2,1)}, f32[8,1536]{1,0:T(8,128)}, f32[8,768]{1,0:T(8,128)}) custom-call(bf16[256,6144]{1,0:T(8,128)(2,1)} %xq_ref.1, bf16[256,6144]{1,0:T(8,128)(2,1)} %xq_ref.1, bf16[1536,1536]{1,0:T(8,128)(2,1)} %wq_ref.1, bf16[1536,256]{1,0:T(8,128)(2,1)} %wk_ref.1, bf16[1536,256]{1,0:T(8,128)(2,1)} %wv_ref.1, ...), custom_call_target="tpu_custom_call" | custom-call | flops 6442450944 | bytes 25165824 | tf_op jit(solution)/shard_map/pallas_call | solution.py:448
  184.6 2.1 %copy.16 = bf16[256,1536]{1,0:T(8,128)(2,1)} copy(bf16[256,1536]{1,0:T(8,128)(2,1)} %get-tuple-element.19) | data formatting | bytes 1572864
  186.7 1.4 copy.17
  188.1 1.3 copy.18
  (3 shorter events, 0.0 us)

commit v3 on v2

--- a/solution.py
+++ b/solution.py
@@ -3,6 +3,7 @@
 
 import jax
 import jax.numpy as jnp
+import numpy as np
 from jax import lax
 from jax.experimental import pallas as pl
 from jax.experimental.pallas import tpu as pltpu
@@ -17,17 +18,13 @@
 neg_big = -1e30
 
 
-def doc_number(token_positions, doc_ends):
-    return jnp.sum((token_positions[:, None] >= doc_ends[None, :]).astype(jnp.int32), axis=1)
-
-
 def whole_kernel(
     n, owners, chunks, presplit,
     x_ref, xq_ref, wq_ref, wk_ref, wv_ref, pack_ref, cot_ref,
-    cos_ref, sin_ref, start_ref, choose_ref,
+    lengths_ref, adapters_ref, rows_ref, cos_hbm, sin_hbm,
     att_ref, down_ref, up_ref,
     out_ref, held, xs, xq, packs, cot, ups, spread, low, mid, kv, bias, gq,
-    give, got, keep, gath,
+    give, got, keep, gath, cos_ref, sin_ref, choose_ref,
     load_sem, x_sem,
     up_send, down_send, y_send, core_send, z_recv, y_recv, core_recv,
     pack_send, pack_recv, low_send, low_recv, mid_send, mid_recv,
@@ -67,6 +64,11 @@
         )
     )
     x_copies.append(pltpu.make_async_copy(cot_ref, cot, load_sem.at[4]))
+    for i, (src, dst) in enumerate(((cos_hbm, cos_ref), (sin_hbm, sin_ref))):
+        first = pl.multiple_of(s * row_count, 8)
+        x_copies.append(
+            pltpu.make_async_copy(src.at[pl.ds(first, row_count), :], dst, load_sem.at[6 + i])
+        )
     copies.append(pltpu.make_async_copy(pack_ref, packs.at[z], load_sem.at[5]))
     for c in copies + x_copies:
         c.start()
@@ -116,18 +118,20 @@
     def from_core(d, gg, c, k):
         return move(d, gg, 1 - s, c, core_send.at[d, c, k], core_recv.at[d, c, k], {"seq": 1 - s})
 
-    def send_own(c):
-        @pl.when(z > 0)
-        def _():
-            to_below(z, c).start()
-
-        @pl.when(z < n - 1)
-        def _():
-            to_above(z, c).start()
+    def send_down(t):
+        @pl.when(jnp.logical_and(z > 0, t < (above + 1) * chunks))
+        def _():
+            to_below(jnp.minimum(z + t // chunks, n - 1), t % chunks).start()
+
+    def send_up(t):
+        @pl.when(jnp.logical_and(z < n - 1, t < (below + 1) * chunks))
+        def _():
+            to_above(jnp.maximum(z - t // chunks, 0), t % chunks).start()
 
     ahead = min(2, chunks)
-    for c in range(ahead):
-        send_own(c)
+    for t in range(ahead):
+        send_down(t)
+        send_up(t)
     pack_copies = [
         pltpu.make_async_remote_copy(
             src_ref=packs.at[z], dst_ref=packs.at[z],
@@ -143,7 +147,21 @@
 
     kpos = lax.broadcasted_iota(jnp.int32, bias.shape, 1)
     qpos = s * row_count + lax.broadcasted_iota(jnp.int32, bias.shape, 0)
-    allowed = jnp.logical_and(kpos <= qpos, kpos >= start_ref[:, :1])
+    tpos = s * row_count + lax.broadcasted_iota(jnp.int32, choose_ref.shape, 1)
+    begin = jnp.zeros(bias.shape, jnp.int32)
+    stored = jnp.zeros(choose_ref.shape, jnp.int32)
+    end = jnp.int32(0)
+    for doc in range(lengths_ref.shape[1]):
+        adapter = adapters_ref[0, doc]
+        row = jnp.int32(0)
+        for i in range(rows_ref.shape[0]):
+            row = row + jnp.where(adapter == i, rows_ref[i], 0)
+        begin = jnp.where(qpos >= end, end, begin)
+        stored = jnp.where(tpos >= end, row, stored)
+        end = end + lengths_ref[0, doc]
+    row_of = lax.broadcasted_iota(jnp.int32, choose_ref.shape, 0) // rank
+    choose_ref[...] = jnp.where(row_of == stored, 1.0, 0.0)
+    allowed = jnp.logical_and(kpos <= qpos, kpos >= begin)
     bias[...] = jnp.where(allowed, 0.0, neg_big)
 
     def owner_copies(buf, send, recv):
@@ -230,30 +248,24 @@
         t = jnp.where(paired, t, t2)
         return jnp.where(up, z + 1 + t // chunks, z - 1 - t // chunks), t % chunks
 
-    def land(d, c, onward, more):
+    def land(d, c):
         to_below(d, c).wait_recv()
-
-        @pl.when(more)
-        def _():
-            onward(d, c).start()
-
-        to_group(d, c).start()
         to_core(d, g, c, 0).start()
 
-    lag = min(2, chunks - 1)
+    lag = min(3, chunks - 1)
 
     def step(t, _):
-        @pl.when(t + ahead < chunks)
-        def _():
-            send_own(jnp.minimum(t + ahead, chunks - 1))
-
         @pl.when(t < above * chunks)
         def _():
-            land(jnp.minimum(z + 1 + t // chunks, n - 1), t % chunks, to_below, z > 0)
+            land(jnp.minimum(z + 1 + t // chunks, n - 1), t % chunks)
 
         @pl.when(t < below * chunks)
         def _():
-            land(jnp.maximum(z - 1 - t // chunks, 0), t % chunks, to_above, z < n - 1)
+            land(jnp.maximum(z - 1 - t // chunks, 0), t % chunks)
+
+        send_down(t + ahead)
+        send_up(t + ahead)
+        to_group(*event(t)).start()
 
         @pl.when(t >= lag)
         def _():
@@ -424,7 +436,7 @@
 
 
 def whole(
-    tokens, query_weight, key_weight, value_weight, pack, cotangent, cosines, sines, starts, choose
+    tokens, query_weight, key_weight, value_weight, pack, cotangent, lengths, adapters, rows
 ):
     n = lax.axis_size("dp")
     owners = lax.axis_size("owner")
@@ -432,8 +444,8 @@
     depth, query_cols = query_weight.shape
     key_cols = key_weight.shape[1]
     cols = query_cols + 2 * key_cols
-    wide = choose.shape[0]
-    rank = wide // n
+    rank = pack.shape[0] // 2
+    wide = n * rank
     quarter = width // owners
     summed = (quarter + query_cols) // 2
     piece = depth // 4
@@ -442,6 +454,12 @@
     split = tokens
     if presplit:
         split = jnp.transpose(tokens.reshape(row_count, n, depth), (1, 0, 2))
+    length = 2 * row_count
+    angles = np.arange(length)[:, None] * rope_base ** (
+        -np.arange(HEAD_SIZE // 2)[None, :] * 2.0 / HEAD_SIZE
+    )
+    cosines = np.concatenate([np.cos(angles), np.cos(angles)], axis=1).astype(np.float32)
+    sines = np.concatenate([-np.sin(angles), np.sin(angles)], axis=1).astype(np.float32)
     dma = pltpu.SemaphoreType.DMA
     bf16 = jnp.bfloat16
     f32 = jnp.float32
@@ -453,7 +471,8 @@
             jax.ShapeDtypeStruct((rank, query_cols // 2), f32),
         ),
         in_specs=[pl.BlockSpec(memory_space=pl.ANY)] * 7
-        + [pl.BlockSpec(memory_space=pltpu.VMEM)] * 4,
+        + [pl.BlockSpec(memory_space=pltpu.SMEM)] * 3
+        + [pl.BlockSpec(memory_space=pl.ANY)] * 2,
         out_specs=(pl.BlockSpec(memory_space=pltpu.VMEM),) * 3,
         scratch_shapes=[
             pltpu.VMEM((row_count, cols), f32),
@@ -473,7 +492,10 @@
             pltpu.VMEM((wide, summed), f32),
             pltpu.VMEM((n, rank, summed), f32),
             pltpu.VMEM((n, rank, summed), f32),
-            dma((6,)),
+            pltpu.VMEM((row_count, HEAD_SIZE), f32),
+            pltpu.VMEM((row_count, HEAD_SIZE), f32),
+            pltpu.VMEM((wide, row_count), f32),
+            dma((8,)),
             dma((n,)),
             dma((n, chunks)),
             dma((n, chunks)),
@@ -503,7 +525,7 @@
         ),
     )(
         split, tokens, query_weight, key_weight, value_weight, pack, cotangent,
-        cosines, sines, starts, choose,
+        lengths, adapters, rows, jnp.asarray(cosines), jnp.asarray(sines),
     )
 
 
@@ -519,39 +541,12 @@
     adapter_up_weight,
     output_cotangent,
 ):
-    row_count = tokens.shape[0]
-    rank = adapter_down_weight.shape[2]
-    adapters = lax.axis_size("dp")
-    doc_count = document_lengths.shape[1]
-    doc_ends = jnp.cumsum(document_lengths[0])
-    own_positions = lax.axis_index("seq") * row_count + jnp.arange(row_count, dtype=jnp.int32)
-    doc_mine = doc_number(own_positions, doc_ends)
-    in_document = doc_mine[:, None] == jnp.arange(doc_count, dtype=jnp.int32)[None, :]
-    starts = jnp.sum(jnp.where(in_document, (doc_ends - document_lengths[0])[None, :], 0), axis=1)
-    starts = jnp.broadcast_to(starts[:, None], (row_count, HEAD_SIZE))
-    adapter_of = jnp.sum(jnp.where(in_document, document_adapter[0][None, :], 0), axis=1)
-    adapter_ids = jnp.arange(adapters, dtype=jnp.int32)
-    stored_row = jnp.sum(
-        jnp.where(adapter_of[:, None] == adapter_ids[None, :], adapter_stored_row[None, :], 0),
-        axis=1,
-    )
-    row_of = jnp.arange(adapters * rank, dtype=jnp.int32) // rank
-    choose = (row_of[:, None] == stored_row[None, :]).astype(jnp.float32)
-    half_width = HEAD_SIZE // 2
-    frequency = rope_base ** (
-        -(jnp.arange(half_width).astype(jnp.float32) * 2.0 / HEAD_SIZE)
-    )
-    angles = own_positions.astype(jnp.float32)[:, None] * frequency[None, :]
-    cosines = jnp.cos(angles)
-    sines = jnp.sin(angles)
-    cosines = jnp.concatenate([cosines, cosines], axis=1)
-    sines = jnp.concatenate([-sines, sines], axis=1)
     line = jnp.concatenate([adapter_up_weight[0], jnp.transpose(adapter_down_weight[0])], axis=1)
     middle = line.shape[1] // 2
     pack = jnp.concatenate([line[:, :middle], line[:, middle:]], axis=0)
     attended, grad_down, grad_up = whole(
         tokens, query_weight, key_weight, value_weight, pack, output_cotangent,
-        cosines, sines, starts, choose,
+        document_lengths, document_adapter, adapter_stored_row,
     )
     return (attended, jnp.transpose(grad_down)[None], grad_up[None])
 

time: 190 us -> 164 us (0.86)
  Pallas kernels: 175 us -> 156 us
  other arithmetic: 7.21 us -> 1.4 us
    pallas_call x1, Pallas kernels: 175 us -> 156 us  [whole(): pl.pallas_call(functools.partial(whole_kernel, n, owners, chunks, prespli...]
where the time goes in v3:
time: 164 us
  Pallas kernels  156 us (95%)
  local copies, waits for them, and re-layouts  5.6 us (3%)
    pallas_call x1, Pallas kernels, whole(): pl.pallas_call(functools.partial(whole_kernel, n, owners, chunks, prespli...  156 us
    unnamed x3, local copies, waits for them, and re-layouts  4.83 us

profile of v3, /device:TPU:0, one launch (start us, length us, event | category | flops | bytes accessed | tf_op | source)
XLA Modules:
  0.0 163.6 jit_solution(8070213403903664538)
XLA Ops:
  0.6 0.8 slice.8
  1.4 1.4 fusion.pack_ref
  2.8 155.9 %shard_map.139 = (bf16[256,1536]{1,0:T(8,128)(2,1)}, f32[8,1536]{1,0:T(8,128)}, f32[8,768]{1,0:T(8,128)}) custom-call(bf16[256,6144]{1,0:T(8,128)(2,1)} %xq_ref.1, bf16[256,6144]{1,0:T(8,128)(2,1)} %xq_ref.1, bf16[1536,1536]{1,0:T(8,128)(2,1)} %wq_ref.1, bf16[1536,256]{1,0:T(8,128)(2,1)} %wk_ref.1, bf16[1536,256]{1,0:T(8,128)(2,1)} %wv_ref.1, ...), custom_call_target="tpu_custom_call" | custom-call | flops 6442450944 | bytes 25165824 | tf_op jit(solution)/shard_map/pallas_call | solution.py:466
  158.7 2.1 %copy.18 = bf16[256,1536]{1,0:T(8,128)(2,1)} copy(bf16[256,1536]{1,0:T(8,128)(2,1)} %get-tuple-element.12) | data formatting | bytes 1572864
  160.8 1.4 copy.19
  162.2 1.3 copy.20

commit v4 on v3

--- a/solution.py
+++ b/solution.py
@@ -27,7 +27,7 @@
     give, got, keep, gath, cos_ref, sin_ref, choose_ref,
     load_sem, x_sem,
     up_send, down_send, y_send, core_send, z_recv, y_recv, core_recv,
-    pack_send, pack_recv, low_send, low_recv, mid_send, mid_recv,
+    pack_send, pack_recv, pack_out, pack_in, low_send, low_recv, mid_send, mid_recv,
     kv_sem, got_sem, gath_send, gath_recv,
 ):
     depth = wq_ref.shape[0]
@@ -132,14 +132,28 @@
     for t in range(ahead):
         send_down(t)
         send_up(t)
+    pack_half = packs.shape[2] // 2
+
+    def pack_part(d, ss):
+        return packs.at[d, :, pl.ds(pl.multiple_of(ss * pack_half, 128), pack_half)]
+
     pack_copies = [
         pltpu.make_async_remote_copy(
-            src_ref=packs.at[z], dst_ref=packs.at[z],
+            src_ref=pack_part(z, s), dst_ref=pack_part(z, s),
             send_sem=pack_send.at[k], recv_sem=pack_recv.at[k],
             device_id={"dp": lax.rem(z + k, n)}, device_id_type=MESH,
         )
         for k in range(1, n)
     ]
+
+    def pack_swap(k, ss):
+        d = lax.rem(z - k + n, n)
+        return pltpu.make_async_remote_copy(
+            src_ref=pack_part(d, ss), dst_ref=pack_part(d, ss),
+            send_sem=pack_out.at[k], recv_sem=pack_in.at[k],
+            device_id={"seq": 1 - s}, device_id_type=MESH,
+        )
+
     for c in pack_copies:
         c.start()
     for c in x_copies:
@@ -188,9 +202,12 @@
     mid_copies = owner_copies(mid, mid_send, mid_recv)
 
     def low_first():
-        for c in pack_copies:
+        for k, c in enumerate(pack_copies):
             c.wait_recv()
-        wide = packs[...].astype(jnp.float32)
+            pack_swap(k + 1, s).start()
+        for k in range(1, n):
+            pack_swap(k, 1 - s).wait_recv()
+        wide = packs[:, :, : (query_cols + width) // 2].astype(jnp.float32)
         ups[...] = wide[:, :rank, :query_cols].reshape(n * rank, query_cols).astype(jnp.bfloat16)
         downs = jnp.concatenate([wide[:, :rank, query_cols:], wide[:, rank:, :]], axis=2)
         downs = downs.reshape(n * rank, width).astype(jnp.bfloat16)
@@ -290,24 +307,38 @@
         multiply(d, False)
 
     def phase(p, _):
-        lax.fori_loop(p * chunks, (p + 1) * chunks, step, 0)
+        middle = p * chunks + lag + 1
+        lax.fori_loop(p * chunks, middle, step, 0)
+        paired = p - 1 < 2 * both
 
         @pl.when(p == 0)
         def _():
             low_first()
 
-        @pl.when(p >= 2)
+        @pl.when(jnp.logical_and(p >= 1, jnp.logical_and(paired, p % 2 == 0)))
         def _():
             finish(jnp.maximum(p - 2, 0))
 
+        @pl.when(
+            jnp.logical_and(p >= 1, jnp.logical_or(jnp.logical_not(paired), p % 2 == 0))
+        )
+        def _():
+            finish(jnp.maximum(p - 1, 0))
+
+        lax.fori_loop(middle, (p + 1) * chunks, step, 0)
         return 0
 
     total = (n - 1) * chunks
     lax.fori_loop(0, n - 1, phase, 0)
     lax.fori_loop(total - lag, total, lambda i, _: (cross(i), 0)[1], 0)
     low_second()
-    for k in range(max(n - 3, 0), n - 1):
-        finish(jnp.int32(k))
+    if n % 2 == 1:
+
+        @pl.when(2 * both == n - 1)
+        def _():
+            finish(jnp.int32(n - 3))
+
+    finish(jnp.int32(n - 2))
 
     half = HEAD_SIZE // 2
 
@@ -358,7 +389,7 @@
         gq[:, cols] = rotate(dot(dscore, keys, 1, 0) * scale, -1).astype(jnp.bfloat16)
         return 0
 
-    lax.fori_loop(0, query_cols // HEAD_SIZE, head, 0)
+    lax.fori_loop(0, query_cols // HEAD_SIZE, head, 0, unroll=3)
 
     mid[0] = chosen(dot(ups[...], gq[...], 1, 1))
     for c in mid_copies:
@@ -408,6 +439,8 @@
     down_ref[...] = total_grad[:, :down_half]
     up_ref[...] = total_grad[:, down_half:]
 
+    for k in range(1, n):
+        pack_swap(k, s).wait_send()
     for c in pack_copies + low_copies + mid_copies + gath_copies + [kv_copy, swap]:
         c.wait_send()
 
@@ -506,6 +539,8 @@
             dma((n, chunks, 2)),
             dma((n,)),
             dma((n,)),
+            dma((n,)),
+            dma((n,)),
             dma((owners,)),
             dma((owners,)),
             dma((owners,)),
@@ -544,6 +579,7 @@
     line = jnp.concatenate([adapter_up_weight[0], jnp.transpose(adapter_down_weight[0])], axis=1)
     middle = line.shape[1] // 2
     pack = jnp.concatenate([line[:, :middle], line[:, middle:]], axis=0)
+    pack = jnp.pad(pack, ((0, 0), (0, -middle % 256)))
     attended, grad_down, grad_up = whole(
         tokens, query_weight, key_weight, value_weight, pack, output_cotangent,
         document_lengths, document_adapter, adapter_stored_row,

time: 164 us -> 158 us (0.963)
  Pallas kernels: 156 us -> 150 us
    pallas_call x1, Pallas kernels: 156 us -> 150 us  [whole(): pl.pallas_call(functools.partial(whole_kernel, n, owners, chunks, prespli...]
where the time goes in v4:
time: 158 us
  Pallas kernels  150 us (95%)
  local copies, waits for them, and re-layouts  5.6 us (4%)
    pallas_call x1, Pallas kernels, whole(): pl.pallas_call(functools.partial(whole_kernel, n, owners, chunks, prespli...  150 us
    unnamed x3, local copies, waits for them, and re-layouts  4.83 us

profile of v4, /device:TPU:0, one launch (start us, length us, event | category | flops | bytes accessed | tf_op | source)
XLA Modules:
  0.0 157.8 jit_solution(15663225032526387265)
XLA Ops:
  0.6 0.8 slice.8
  1.4 1.4 fusion.pack_ref
  2.8 150.2 %shard_map.139 = (bf16[256,1536]{1,0:T(8,128)(2,1)}, f32[8,1536]{1,0:T(8,128)}, f32[8,768]{1,0:T(8,128)}) custom-call(bf16[256,6144]{1,0:T(8,128)(2,1)} %xq_ref.1, bf16[256,6144]{1,0:T(8,128)(2,1)} %xq_ref.1, bf16[1536,1536]{1,0:T(8,128)(2,1)} %wq_ref.1, bf16[1536,256]{1,0:T(8,128)(2,1)} %wk_ref.1, bf16[1536,256]{1,0:T(8,128)(2,1)} %wv_ref.1, ...), custom_call_target="tpu_custom_call" | custom-call | flops 6442450944 | bytes 25165824 | tf_op jit(solution)/shard_map/pallas_call | solution.py:499
  153.0 2.1 %copy.18 = bf16[256,1536]{1,0:T(8,128)(2,1)} copy(bf16[256,1536]{1,0:T(8,128)(2,1)} %get-tuple-element.12) | data formatting | bytes 1572864
  155.1 1.4 copy.19
  156.5 1.3 copy.20

commit v5 on v4

--- a/solution.py
+++ b/solution.py
@@ -315,6 +315,10 @@
         def _():
             low_first()
 
+        @pl.when(p == min(1, n - 2))
+        def _():
+            low_second()
+
         @pl.when(jnp.logical_and(p >= 1, jnp.logical_and(paired, p % 2 == 0)))
         def _():
             finish(jnp.maximum(p - 2, 0))
@@ -331,7 +335,6 @@
     total = (n - 1) * chunks
     lax.fori_loop(0, n - 1, phase, 0)
     lax.fori_loop(total - lag, total, lambda i, _: (cross(i), 0)[1], 0)
-    low_second()
     if n % 2 == 1:
 
         @pl.when(2 * both == n - 1)
@@ -389,7 +392,7 @@
         gq[:, cols] = rotate(dot(dscore, keys, 1, 0) * scale, -1).astype(jnp.bfloat16)
         return 0
 
-    lax.fori_loop(0, query_cols // HEAD_SIZE, head, 0, unroll=3)
+    lax.fori_loop(0, query_cols // HEAD_SIZE, head, 0, unroll=6)
 
     mid[0] = chosen(dot(ups[...], gq[...], 1, 1))
     for c in mid_copies:

time: 158 us -> 157 us (level)
  no operation moved by 1% of the time
where the time goes in v5:
time: 157 us
  Pallas kernels  149 us (95%)
  local copies, waits for them, and re-layouts  5.6 us (4%)
    pallas_call x1, Pallas kernels, whole(): pl.pallas_call(functools.partial(whole_kernel, n, owners, chunks, prespli...  149 us
    unnamed x3, local copies, waits for them, and re-layouts  4.83 us

profile of v5, /device:TPU:0, one launch (start us, length us, event | category | flops | bytes accessed | tf_op | source)
XLA Modules:
  0.0 156.9 jit_solution(9304860897112772087)
XLA Ops:
  0.6 0.8 slice.8
  1.4 1.4 fusion.pack_ref
  2.8 149.2 %shard_map.139 = (bf16[256,1536]{1,0:T(8,128)(2,1)}, f32[8,1536]{1,0:T(8,128)}, f32[8,768]{1,0:T(8,128)}) custom-call(bf16[256,6144]{1,0:T(8,128)(2,1)} %xq_ref.1, bf16[256,6144]{1,0:T(8,128)(2,1)} %xq_ref.1, bf16[1536,1536]{1,0:T(8,128)(2,1)} %wq_ref.1, bf16[1536,256]{1,0:T(8,128)(2,1)} %wk_ref.1, bf16[1536,256]{1,0:T(8,128)(2,1)} %wv_ref.1, ...), custom_call_target="tpu_custom_call" | custom-call | flops 6442450944 | bytes 25165824 | tf_op jit(solution)/shard_map/pallas_call | solution.py:502
  152.0 2.1 %copy.18 = bf16[256,1536]{1,0:T(8,128)(2,1)} copy(bf16[256,1536]{1,0:T(8,128)(2,1)} %get-tuple-element.12) | data formatting | bytes 1572864
  154.1 1.4 copy.19
  155.5 1.3 copy.20
